TPU v7x, 32 devices: a whole 2x2x4 slice. The times are simulated.
32 devices in a mesh: dp: 8 (over z, core), expert: 4 (over y, x).
Axes of the slice: x: 2, y: 2, z: 4, core: 2. Of those that a mesh axis runs over, the one named last changes fastest.
Arguments:
- tokens: bfloat16 [512, 4096], P('expert', 'dp'), may hold values from -6 to 6
- cotangent: bfloat16 [512, 4096], P('expert', 'dp'), may hold values from -2.25 to 2.25
- routes: int32 [512, 2], P('expert'), may hold values from 0 to 15, all different within a row; in each aligned block of 128 rows (0 to 127, 128 to 255, ...) at most 40 rows name the same one
- gates: float32 [512, 2], P('expert'), may hold values from 0.05 to 1
- expert_weights: bfloat16 [16, 3, 2048, 4096], P('expert', None, 'dp'), may hold values from -0.09375 to 0.09375
Outputs:
- weight_grads: bfloat16 [16, 3, 2048, 4096], P('expert', None, 'dp')
Inputs may be any that keep to these rules, and one draw needn't show every extreme that they name: Each row names 2 different experts; within the 128 rows of one index of the expert axis no expert is named by more than 40 routes.
All inputs are finite; a program needn't handle non-finite values.
Results may differ from a plain program's by a relative error of at most 0.0057.
Values may be sent and summed in bfloat16 or wider, within the bound.
A program may use at most 128 MiB of HBM per device.

v0:
```python
import jax
import jax.numpy as jnp
from jax import lax
from jax.sharding import PartitionSpec as P

CAP = 40


def block_terms(input_rows, scaled, weights):
    along = (((1,), (1,)), ((), ()))
    gate_part = lax.dot_general(input_rows, weights[0], along, preferred_element_type=jnp.float32)
    up_part = lax.dot_general(input_rows, weights[1], along, preferred_element_type=jnp.float32)
    sigmoid_part = jax.nn.sigmoid(gate_part)
    hidden = (gate_part * sigmoid_part * up_part).astype(jnp.bfloat16)
    back_hidden = lax.dot_general(scaled, weights[2], along, preferred_element_type=jnp.float32)
    derivative = sigmoid_part * (1.0 + gate_part * (1.0 - sigmoid_part))
    pre_gate = (back_hidden * up_part * derivative).astype(jnp.bfloat16)
    pre_up = (back_hidden * gate_part * sigmoid_part).astype(jnp.bfloat16)
    contract = (((0,), (0,)), ((), ()))
    gate_grads = lax.dot_general(pre_gate, input_rows, contract, preferred_element_type=jnp.float32)
    up_grads = lax.dot_general(pre_up, input_rows, contract, preferred_element_type=jnp.float32)
    down_grads = lax.dot_general(hidden, scaled, contract, preferred_element_type=jnp.float32)
    return jnp.stack([gate_grads, up_grads, down_grads], axis=0)


def pack_rows(tokens, cotangent, gates_flat, source_of, route_count, per_token):
    filled = source_of < route_count
    clamped = jnp.minimum(source_of, route_count - 1)
    token_index = clamped // per_token
    input_rows = jnp.where(
        filled[:, None], jnp.take(tokens, token_index, axis=0), jnp.zeros((), tokens.dtype)
    )
    weight = jnp.where(filled, jnp.take(gates_flat, clamped), jnp.zeros((), jnp.float32))
    scaled = (
        weight[:, None] * jnp.take(cotangent, token_index, axis=0).astype(jnp.float32)
    ).astype(jnp.bfloat16)
    return (input_rows, scaled)


def expert_sum(received_rows, received_scaled, weights, row_index, filled_rows):
    step_rows = 128
    block_total = (filled_rows + step_rows - 1) // step_rows
    start_sum = jnp.zeros(weights.shape, jnp.float32)

    def one_block(block_index, running_sum):
        first_row = block_index * step_rows
        chosen = lax.dynamic_slice_in_dim(row_index, first_row, step_rows)
        filled = first_row + jnp.arange(step_rows, dtype=jnp.int32) < filled_rows
        input_rows = jnp.where(
            filled[:, None],
            jnp.take(received_rows, chosen, axis=0),
            jnp.zeros((), received_rows.dtype),
        )
        scaled = jnp.where(
            filled[:, None],
            jnp.take(received_scaled, chosen, axis=0),
            jnp.zeros((), received_scaled.dtype),
        )
        return running_sum + block_terms(input_rows, scaled, weights)

    return lax.fori_loop(0, block_total, one_block, start_sum)


def per_device(tokens, cotangent, routes, gates, expert_weights):
    per_token = routes.shape[1]
    local_count = expert_weights.shape[0]
    groups = lax.axis_size("expert")
    expert_total = local_count * groups
    own_index = lax.axis_index("expert")
    routed = routes.reshape(-1)
    route_count = routed.shape[0]
    gates_flat = gates.reshape(-1)
    matches = (routed[:, None] == jnp.arange(expert_total, dtype=jnp.int32)[None, :]).astype(
        jnp.int32
    )
    own_counts = jnp.sum(matches, axis=0)
    earlier = jnp.cumsum(matches, axis=0) - matches
    position = jnp.sum(earlier * matches, axis=1)
    own_row = (jnp.arange(groups, dtype=jnp.int32) == own_index).astype(jnp.int32)
    load_table = lax.psum(own_row[:, None] * own_counts[None, :], "expert")
    travels = routed >= 0
    target = jnp.where(travels, routed * CAP + position, expert_total * CAP)
    source_of = (
        jnp.full((expert_total * CAP,), route_count, jnp.int32)
        .at[target]
        .set(jnp.arange(route_count, dtype=jnp.int32), mode="drop")
    )
    send_rows, send_scaled = pack_rows(
        tokens, cotangent, gates_flat, source_of, route_count, per_token
    )
    arrived_rows, arrived_scaled = (
        lax.all_to_all(send_rows, "expert", split_axis=0, concat_axis=0, tiled=True),
        lax.all_to_all(send_scaled, "expert", split_axis=0, concat_axis=0, tiled=True),
    )
    received_rows, received_scaled = (
        lax.all_gather(arrived_rows, "dp", axis=1, tiled=True),
        lax.all_gather(arrived_scaled, "dp", axis=1, tiled=True),
    )
    length = -(-(groups * CAP) // 128) * 128
    places = jnp.arange(length, dtype=jnp.int32)
    grads_list = []
    for local_slot in range(local_count):
        expert_id = own_index * local_count + local_slot
        per_source = jnp.take(load_table, expert_id, axis=1)
        running = jnp.cumsum(per_source)
        opening = running - per_source
        filled_rows = running[groups - 1]
        source = jnp.minimum(
            jnp.sum((running[None, :] <= places[:, None]).astype(jnp.int32), axis=1), groups - 1
        )
        offset = jnp.clip(places - opening[source], 0, CAP - 1)
        row_index = source * (local_count * CAP) + local_slot * CAP + offset
        grads_list.append(
            expert_sum(
                received_rows, received_scaled, expert_weights[local_slot], row_index, filled_rows
            )
        )
    grads = jnp.stack(grads_list, axis=0)
    return grads.astype(jnp.bfloat16)


def solution(mesh):
    return jax.shard_map(
        per_device,
        mesh=mesh,
        in_specs=(
            P("expert", "dp"),
            P("expert", "dp"),
            P("expert", None),
            P("expert", None),
            P("expert", None, "dp", None),
        ),
        out_specs=P("expert", None, "dp", None),
        check_vma=False,
    )
```

profile of v0, /device:TPU:5, one launch (start us, length us, event | category | flops | bytes accessed | tf_op | source)
XLA Modules:
  0.0 398.7 jit_solution(13828866259897410453)
XLA Ops:
  28.1 11.0 %all_to_all.24 = bf16[4,160,512]{2,1,0:T(8,128)(2,1)} all-to-all(bf16[4,160,512]{2,1,0:T(8,128)(2,1)S(1)} %bitcast.188), channel_id=1, replica_groups=mesh['dp'=8,'expert'=4] {'expert'}, dimensions={0} | all-to-all | bytes 1310720 | tf_op jit(solution)/shard_map/all_to_all | solution.py:93
  42.2 9.5 %all_to_all.25 = bf16[4,160,512]{2,1,0:T(8,128)(2,1)} all-to-all(bf16[4,160,512]{2,1,0:T(8,128)(2,1)S(1)} %bitcast.187), channel_id=1, replica_groups=mesh['dp'=8,'expert'=4] {'expert'}, dimensions={0} | all-to-all | bytes 1310720 | tf_op jit(solution)/shard_map/all_to_all | solution.py:92
  69.1 17.9 %slice_bitcast_fusion.3 = (bf16[3,256,4096]{2,1,0:T(8,128)(2,1)}, bf16[3,256,4096]{2,1,0:T(8,128)(2,1)}, bf16[3,256,4096]{2,1,0:T(8,128)(2,1)}, bf16[3,256,4096]{2,1,0:T(8,128)(2,1)}) fusion(bf16[4,3,256,4096]{3,2,1,0:T(8,128)(2,1)} %param.23), kind=kLoop, calls=%fused_computation.136 | loop fusion | bytes 50331648 | tf_op jit(solution)/shard_map/squeeze | solution.py:115
  87.0 11.9 %all-gather.3.cloned.1.call-done = bf16[640,4096]{1,0:T(8,128)(2,1)} async-done(((bf16[640,512]{1,0:T(8,128)(2,1)}), bf16[640,4096]{1,0:T(8,128)(2,1)}) %all-gather.3.cloned.1.call-update) | async-done | bytes 5242896 | tf_op jit(solution)/shard_map/all_gather | solution.py:97
  98.9 56.5 %all-gather.5.cloned.1.call-done = bf16[640,4096]{1,0:T(8,128)(2,1)} async-done(((bf16[640,512]{1,0:T(8,128)(2,1)}), bf16[640,4096]{1,0:T(8,128)(2,1)}) %all-gather.5.cloned.1.call-update) | async-done | bytes 5242896 | tf_op jit(solution)/shard_map/all_gather | solution.py:96
  155.4 6.3 %broadcast.238.clone = f32[3,256,4096]{2,1,0:T(8,128)} broadcast(f32[]{:T(128)} %constant.175.clone.1), dimensions={} | broadcast | bytes 12582916 | tf_op jit(solution)/shard_map/broadcast.17
  161.7 64.0 %while.44 = (s32[]{:T(128)}, f32[3,256,4096]{2,1,0:T(8,128)}, s32[]{:T(128)}, s32[]{:T(128)}, s32[256]{0:T(256)S(1)}, /*index=5*/bf16[640,4096]{1,0:T(8,128)(2,1...) while((s32[]{:T(128)}, f32[3,256,4096]{2,1,0:T(8,128)}, ...), condition=%wide.region_21.25_spmd, body=%wide.region_20.24_spmd.sunk | while | flops 1627064320 | bytes 68428216 | solution.py:61
  162.9 5.4 %gather_fusion.6 = bf16[128,4096]{1,0:T(8,128)(2,1)S(1)} fusion(bf16[640,4096]{1,0:T(8,128)(2,1)} %get-tuple-element.560, s32[1024]{0:T(1024)S(1)} %pad_clamp_fusion.13), kind=kCustom, calls=%fused_computation.9.clone.clone.1 | custom fusion | bytes 2097664 | tf_op jit(solution)/shard_map/while/body/jit(_take)/gather | solution.py:51
  173.2 5.4 %gather_fusion.7 = bf16[128,4096]{1,0:T(8,128)(2,1)S(1)} fusion(bf16[640,4096]{1,0:T(8,128)(2,1)} %get-tuple-element.558, s32[1024]{0:T(1024)S(1)} %pad_clamp_fusion.13), kind=kCustom, calls=%fused_computation.8.clone.clone.1 | custom fusion | bytes 2097664 | tf_op jit(solution)/shard_map/while/body/jit(_take)/gather | solution.py:56
  183.4 10.6 %maximum_add_fusion.11 = f32[3,256,4096]{2,1,0:T(8,128)} fusion(f32[3,256,4096]{2,1,0:T(8,128)} %get-tuple-element.542, f32[1,256,4096]{2,1,0:T(8,128)S(1)} %convolution_bitcast_fusion.33, f32[1,256,4096]{2,1,0:T(8,128)S(1)} %convolution_bitcast_fusion.34, f32[1,256,4096]{2,1,0:T(8,128)S(1)} %convolution_bitcast_fusion.35), kind=kLoop, calls=%fused_computation.99.clone.1 | loop fusion | flops 9437184 | bytes 37748736 | tf_op jit(solution)/shard_map/while/body/add | solution.py:59
  194.7 5.4 %gather_fusion.6 = bf16[128,4096]{1,0:T(8,128)(2,1)S(1)} fusion(bf16[640,4096]{1,0:T(8,128)(2,1)} %get-tuple-element.560, s32[1024]{0:T(1024)S(1)} %pad_clamp_fusion.13), kind=kCustom, calls=%fused_computation.9.clone.clone.1 | custom fusion | bytes 2097664 | tf_op jit(solution)/shard_map/while/body/jit(_take)/gather | solution.py:51
  205.0 5.4 %gather_fusion.7 = bf16[128,4096]{1,0:T(8,128)(2,1)S(1)} fusion(bf16[640,4096]{1,0:T(8,128)(2,1)} %get-tuple-element.558, s32[1024]{0:T(1024)S(1)} %pad_clamp_fusion.13), kind=kCustom, calls=%fused_computation.8.clone.clone.1 | custom fusion | bytes 2097664 | tf_op jit(solution)/shard_map/while/body/jit(_take)/gather | solution.py:56
  215.1 10.6 %maximum_add_fusion.11 = f32[3,256,4096]{2,1,0:T(8,128)} fusion(f32[3,256,4096]{2,1,0:T(8,128)} %get-tuple-element.542, f32[1,256,4096]{2,1,0:T(8,128)S(1)} %convolution_bitcast_fusion.33, f32[1,256,4096]{2,1,0:T(8,128)S(1)} %convolution_bitcast_fusion.34, f32[1,256,4096]{2,1,0:T(8,128)S(1)} %convolution_bitcast_fusion.35), kind=kLoop, calls=%fused_computation.99.clone.1 | loop fusion | flops 9437184 | bytes 37748736 | tf_op jit(solution)/shard_map/while/body/add | solution.py:59
  225.7 8.2 %convert_bitcast_fusion = bf16[1,3,256,4096]{3,2,1,0:T(8,128)(2,1)} fusion(f32[3,256,4096]{2,1,0:T(8,128)} %get-tuple-element.183), kind=kLoop, calls=%fused_computation.129 | loop fusion | flops 3145728 | bytes 18874368 | tf_op jit(solution)/shard_map/stack | solution.py:118
  233.9 6.3 %broadcast.238.clone.1 = f32[3,256,4096]{2,1,0:T(8,128)} broadcast(f32[]{:T(128)} %constant.175.clone.1), dimensions={} | broadcast | bytes 12582916 | tf_op jit(solution)/shard_map/broadcast.17
  240.2 31.8 %while.43 = (s32[]{:T(128)}, f32[3,256,4096]{2,1,0:T(8,128)}, s32[]{:T(128)}, s32[]{:T(128)}, s32[256]{0:T(256)S(1)}, /*index=5*/bf16[640,4096]{1,0:T(8,128)(2,1...) while((s32[]{:T(128)}, f32[3,256,4096]{2,1,0:T(8,128)}, ...), condition=%wide.region_17.21_spmd, body=%wide.region_16.20_spmd.sunk | while | flops 1627064320 | bytes 68428216 | solution.py:61
  241.1 5.4 %gather_fusion.4 = bf16[128,4096]{1,0:T(8,128)(2,1)S(1)} fusion(bf16[640,4096]{1,0:T(8,128)(2,1)} %get-tuple-element.596, s32[1024]{0:T(1024)S(1)} %pad_clamp_fusion.12), kind=kCustom, calls=%fused_computation.7.clone.clone.1 | custom fusion | bytes 2097664 | tf_op jit(solution)/shard_map/while/body/jit(_take)/gather | solution.py:51
  261.5 10.6 %maximum_add_fusion.10 = f32[3,256,4096]{2,1,0:T(8,128)} fusion(f32[3,256,4096]{2,1,0:T(8,128)} %get-tuple-element.578, f32[1,256,4096]{2,1,0:T(8,128)S(1)} %convolution_bitcast_fusion.30, f32[1,256,4096]{2,1,0:T(8,128)S(1)} %convolution_bitcast_fusion.31, f32[1,256,4096]{2,1,0:T(8,128)S(1)} %convolution_bitcast_fusion.32), kind=kLoop, calls=%fused_computation.70.clone.1 | loop fusion | flops 9437184 | bytes 37748736 | tf_op jit(solution)/shard_map/while/body/add | solution.py:59
  272.1 8.1 %convert_bitcast_fusion.1 = bf16[1,3,256,4096]{3,2,1,0:T(8,128)(2,1)} fusion(f32[3,256,4096]{2,1,0:T(8,128)} %get-tuple-element.182), kind=kLoop, calls=%fused_computation.131 | loop fusion | flops 3145728 | bytes 18874368 | tf_op jit(solution)/shard_map/stack | solution.py:118
  280.2 6.3 %broadcast.238.clone.2 = f32[3,256,4096]{2,1,0:T(8,128)} broadcast(f32[]{:T(128)} %constant.175.clone.1), dimensions={} | broadcast | bytes 12582916 | tf_op jit(solution)/shard_map/broadcast.17
  286.5 31.9 %while.42 = (s32[]{:T(128)}, f32[3,256,4096]{2,1,0:T(8,128)}, s32[]{:T(128)}, s32[]{:T(128)}, s32[256]{0:T(256)S(1)}, /*index=5*/bf16[640,4096]{1,0:T(8,128)(2,1...) while((s32[]{:T(128)}, f32[3,256,4096]{2,1,0:T(8,128)}, ...), condition=%wide.region_13.17_spmd, body=%wide.region_12.16_spmd.sunk | while | flops 1627064320 | bytes 68428216 | solution.py:61
  287.4 5.4 %gather_fusion.2 = bf16[128,4096]{1,0:T(8,128)(2,1)S(1)} fusion(bf16[640,4096]{1,0:T(8,128)(2,1)} %get-tuple-element.632, s32[1024]{0:T(1024)S(1)} %pad_clamp_fusion.11), kind=kCustom, calls=%fused_computation.5.clone.clone.1 | custom fusion | bytes 2097664 | tf_op jit(solution)/shard_map/while/body/jit(_take)/gather | solution.py:51
  297.7 5.4 %gather_fusion.3 = bf16[128,4096]{1,0:T(8,128)(2,1)S(1)} fusion(bf16[640,4096]{1,0:T(8,128)(2,1)} %get-tuple-element.630, s32[1024]{0:T(1024)S(1)} %pad_clamp_fusion.11), kind=kCustom, calls=%fused_computation.4.clone.clone.1 | custom fusion | bytes 2097664 | tf_op jit(solution)/shard_map/while/body/jit(_take)/gather | solution.py:56
  307.9 10.6 %maximum_add_fusion.9 = f32[3,256,4096]{2,1,0:T(8,128)} fusion(f32[3,256,4096]{2,1,0:T(8,128)} %get-tuple-element.614, f32[1,256,4096]{2,1,0:T(8,128)S(1)} %convolution_bitcast_fusion.27, f32[1,256,4096]{2,1,0:T(8,128)S(1)} %convolution_bitcast_fusion.28, f32[1,256,4096]{2,1,0:T(8,128)S(1)} %convolution_bitcast_fusion.29), kind=kLoop, calls=%fused_computation.41.clone.1 | loop fusion | flops 9437184 | bytes 37748736 | tf_op jit(solution)/shard_map/while/body/add | solution.py:59
  318.4 8.1 %convert_bitcast_fusion.2 = bf16[1,3,256,4096]{3,2,1,0:T(8,128)(2,1)} fusion(f32[3,256,4096]{2,1,0:T(8,128)} %get-tuple-element.181), kind=kLoop, calls=%fused_computation.133 | loop fusion | flops 3145728 | bytes 18874368 | tf_op jit(solution)/shard_map/stack | solution.py:118
  326.6 6.3 %broadcast.238.clone.3 = f32[3,256,4096]{2,1,0:T(8,128)} broadcast(f32[]{:T(128)} %constant.175.clone.1), dimensions={} | broadcast | bytes 12582916 | tf_op jit(solution)/shard_map/broadcast.17
  332.9 31.9 %while.41 = (s32[]{:T(128)}, f32[3,256,4096]{2,1,0:T(8,128)}, s32[]{:T(128)}, s32[]{:T(128)}, s32[256]{0:T(256)S(1)}, /*index=5*/bf16[640,4096]{1,0:T(8,128)(2,1...) while((s32[]{:T(128)}, f32[3,256,4096]{2,1,0:T(8,128)}, ...), condition=%wide.region_9.13_spmd, body=%wide.region_8.12_spmd.sunk | while | flops 1627064320 | bytes 68428216 | solution.py:61
  333.9 5.4 %gather_fusion = bf16[128,4096]{1,0:T(8,128)(2,1)S(1)} fusion(bf16[640,4096]{1,0:T(8,128)(2,1)} %get-tuple-element.668, s32[1024]{0:T(1024)S(1)} %pad_clamp_fusion.10), kind=kCustom, calls=%fused_computation.3.clone.clone.1 | custom fusion | bytes 2097664 | tf_op jit(solution)/shard_map/while/body/jit(_take)/gather | solution.py:51
  344.1 5.4 %gather_fusion.1 = bf16[128,4096]{1,0:T(8,128)(2,1)S(1)} fusion(bf16[640,4096]{1,0:T(8,128)(2,1)} %get-tuple-element.666, s32[1024]{0:T(1024)S(1)} %pad_clamp_fusion.10), kind=kCustom, calls=%fused_computation.1.clone.clone.1 | custom fusion | bytes 2097664 | tf_op jit(solution)/shard_map/while/body/jit(_take)/gather | solution.py:56
  354.3 10.6 %maximum_add_fusion.8 = f32[3,256,4096]{2,1,0:T(8,128)} fusion(f32[3,256,4096]{2,1,0:T(8,128)} %get-tuple-element.650, f32[1,256,4096]{2,1,0:T(8,128)S(1)} %convolution_bitcast_fusion.24, f32[1,256,4096]{2,1,0:T(8,128)S(1)} %convolution_bitcast_fusion.25, f32[1,256,4096]{2,1,0:T(8,128)S(1)} %convolution_bitcast_fusion.26), kind=kLoop, calls=%fused_computation.12.clone.1 | loop fusion | flops 9437184 | bytes 37748736 | tf_op jit(solution)/shard_map/while/body/add | solution.py:59
  364.8 8.3 %convert_bitcast_fusion.3 = bf16[1,3,256,4096]{3,2,1,0:T(8,128)(2,1)} fusion(f32[3,256,4096]{2,1,0:T(8,128)} %get-tuple-element.180), kind=kLoop, calls=%fused_computation.135 | loop fusion | flops 3145728 | bytes 18874368 | tf_op jit(solution)/shard_map/stack | solution.py:118
  373.2 18.2 %pad_maximum_fusion = bf16[4,3,256,4096]{3,2,1,0:T(8,128)(2,1)} fusion(bf16[1,3,256,4096]{3,2,1,0:T(8,128)(2,1)} %convert_bitcast_fusion, bf16[1,3,256,4096]{3,2,1,0:T(8,128)(2,1)} %convert_bitcast_fusion.1, bf16[1,3,256,4096]{3,2,1,0:T(8,128)(2,1)S(1)} %copy-done.3, bf16[1,3,256,4096]{3,2,1,0:T(8,128)(2,1)} %convert_bitcast_fusion.3), kind=kLoop, calls=%fused_computation.128 | loop fusion | flops 37748736 | bytes 50331648 | tf_op jit(solution)/shard_map/stack | solution.py:118
  (123 shorter events, 96.3 us)
Async XLA Ops:
  6.5 18.5 %copy-start = (bf16[128,512]{1,0:T(8,128)(2,1)S(1)}, bf16[128,512]{1,0:T(8,128)(2,1)}, u32[]{:S(2)}) copy-start(bf16[128,512]{1,0:T(8,128)(2,1)} %param.20) | copy-start | bytes 393220
  6.5 92.3 %all-gather.3.cloned.1.call-start = ((), (), s32[]{:S(2)}) async-start(), calls=%async_computation.2 | async-start | bytes 5898240 | tf_op jit(solution)/shard_map/all_gather | solution.py:97
  20.7 18.4 %copy-start.2 = (bf16[128,512]{1,0:T(8,128)(2,1)S(1)}, bf16[128,512]{1,0:T(8,128)(2,1)}, u32[]{:S(2)}) copy-start(bf16[128,512]{1,0:T(8,128)(2,1)} %param.19) | copy-start | bytes 393220
  39.1 116.3 %all-gather.5.cloned.1.call-start = ((), (), s32[]{:S(2)}) async-start(), calls=%async_computation.3 | async-start | bytes 5898240 | tf_op jit(solution)/shard_map/all_gather | solution.py:96
  233.9 6.3 %copy-start.6 = (s32[256]{0:T(256)S(1)}, s32[256]{0:T(256)}, u32[]{:S(2)}) copy-start(s32[256]{0:T(256)} %clamp_add_fusion.1) | copy-start | bytes 3076
  280.2 6.3 %copy-start.5 = (s32[256]{0:T(256)S(1)}, s32[256]{0:T(256)}, u32[]{:S(2)}) copy-start(s32[256]{0:T(256)} %clamp_add_fusion.2) | copy-start | bytes 3076
  326.6 6.3 %copy-start.4 = (s32[256]{0:T(256)S(1)}, s32[256]{0:T(256)}, u32[]{:S(2)}) copy-start(s32[256]{0:T(256)} %clamp_add_fusion.3) | copy-start | bytes 3076
  364.8 8.4 %copy-start.3 = (bf16[1,3,256,4096]{3,2,1,0:T(8,128)(2,1)S(1)}, bf16[1,3,256,4096]{3,2,1,0:T(8,128)(2,1)}, u32[]{:S(2)}) copy-start(bf16[1,3,256,4096]{3,2,1,0:T(8,128)(2,1)} %convert_bitcast_fusion.2) | copy-start | bytes 18874372
  373.2 18.2 %copy-start.1 = (bf16[128,512]{1,0:T(8,128)(2,1)S(1)}, bf16[128,512]{1,0:T(8,128)(2,1)}, u32[]{:S(2)}) copy-start(bf16[128,512]{1,0:T(8,128)(2,1)} %param.20) | copy-start | bytes 393220
Sparse Core Ops, SparseCore 0:
  39.2 59.6 all-gather.2
  100.5 54.8 all-gather.4
where the time goes:
time: 406 us; the launch traced here: 399 us
  other arithmetic  123 us (30%)
  local copies, waits for them, and re-layouts  116 us (29%)
  waiting for transfers between devices  68.4 us (17%)
  matrix products  48.2 us (12%)
  blocking collectives  24.7 us (6%)
  between operations  16.8 us (4%)
    all_gather x1, waiting for transfers between devices, per_device(): lax.all_gather(arrived_rows, 'dp', axis=1, tiled=True)  56.5 us
    add x5, other arithmetic, one_block(): return running_sum + block_terms(input_rows, scaled, weights)  52.8 us
    another operation x5, other arithmetic, per_device(): grads = jnp.stack(grads_list, axis=0)  51 us
    gather x5, local copies, waits for them, and re-layouts, one_block(): jnp.take(received_rows, chosen, axis=0)  26.8 us
    gather x5, local copies, waits for them, and re-layouts, one_block(): jnp.take(received_scaled, chosen, axis=0)  26.8 us
    another operation x5, local copies, waits for them, and re-layouts  25.4 us
    squeeze x1, local copies, waits for them, and re-layouts, per_device(): expert_weights[local_slot]  17.9 us
    dot_general x5, matrix products, block_terms(): lax.dot_general(scaled, weights[2], along, preferred_element_type=jnp.flo...  12.2 us
  transfers between devices with their start and end apart: 2, of which 2 were waited for; matrix products, arithmetic and copies ran while one was open for 9% of the time, Pallas kernels for 0%

commit v1 on v0

v1 whole, which is shorter than its diff:
```python
import functools

import jax
import jax.numpy as jnp
from jax import lax
from jax.experimental import pallas as pl
from jax.experimental.pallas import tpu as pltpu
from jax.sharding import PartitionSpec as P

CAP = 40
CORES = 2
MESH = pl.DeviceIdType.MESH


def exchange_kernel(
    sizes, tok_ref, cot_ref, meta_ref, w_ref,
    rows_ref, pre_ref,
    buf, metab, wbuf, sel, gsel, rows, acc,
    rsem, zsem, esem, bsem, msem_r, msem_s, osem, wsem, rowsem,
):
    chips, groups, local, per_token, length = sizes
    stages = groups.bit_length() - 1
    dp = lax.axis_index("dp")
    own = lax.axis_index("expert")
    z, core = dp // CORES, dp % CORES
    other = 1 - core
    tokens_each, features = tok_ref.shape

    def peer(z_to, core_to, group_to):
        return (z_to * CORES + core_to, group_to)

    def across(index, bit):
        return index + bit - 2 * bit * ((index // bit) % 2)

    def mirror(mask):
        result = own
        for place in range(stages):
            if mask >> place & 1:
                result = across(result, 1 << place)
        return result

    own_copies = [
        pltpu.make_async_copy(ref, buf.at[core, a, z, own], osem.at[a])
        for a, ref in enumerate((tok_ref, cot_ref))
    ] + [pltpu.make_async_copy(meta_ref, metab.at[own], osem.at[2])]
    for copy in own_copies:
        copy.start()

    greeted = [
        peer(lax.rem(z + 1, chips), core, own),
        peer(lax.rem(z + chips - 1, chips), core, own),
        peer(z, other, own),
    ] + [peer(z, core, mirror(mask)) for mask in range(1, groups)]
    barrier = pltpu.get_barrier_semaphore()
    for device in greeted:
        pl.semaphore_signal(barrier, inc=1, device_id=device, device_id_type=MESH)
    pl.semaphore_wait(barrier, len(greeted))
    for copy in own_copies:
        copy.wait()

    def send(c, a, zz, s, sem, device):
        return pltpu.make_async_remote_copy(
            src_ref=buf.at[c, a, zz, s], dst_ref=buf.at[c, a, zz, s],
            send_sem=sem, recv_sem=rsem.at[c, a, zz, s],
            device_id=device, device_id_type=MESH,
        )

    def arrived(c, a, zz, s):
        pltpu.make_async_copy(
            buf.at[c, a, zz, s], buf.at[c, a, zz, s], rsem.at[c, a, zz, s]
        ).wait()

    def to_sibling(a, zz, s):
        send(core, a, zz, s, bsem, peer(z, other, own)).start()

    def bit_of(a, stage):
        return 1 << ((stage + a) % stages)

    def mask_list(a, stage):
        masks = [0]
        for earlier in range(stage):
            masks = masks + [mask ^ bit_of(a, earlier) for mask in masks]
        return masks

    def fresh_masks(a, stage):
        return [mask ^ bit_of(a, stage) for mask in mask_list(a, stage)]

    def nearest(k):
        m = jnp.where(2 * z < chips, z, chips - 1 - z)
        side = jnp.where(k % 2 == 1, z - (k + 1) // 2, z + k // 2)
        rest = jnp.where(2 * z < chips, k, chips - 1 - k)
        return jnp.where(k <= 2 * m, side, rest)

    def z_send(zz, a, upward):
        return send(
            core, a, zz, own, zsem.at[a, zz, 0 if upward else 1],
            peer(z + 1 if upward else z - 1, core, own),
        )

    def z_forward(zz, first):
        for a in range(2):
            if not first:
                arrived(core, a, zz, own)

            @pl.when((zz <= z) & (z < chips - 1))
            def _():
                z_send(zz, a, True).start()

            @pl.when((zz >= z) & (z > 0))
            def _():
                z_send(zz, a, False).start()

            to_sibling(a, zz, own)

    def stage_send(k, stage):
        zz = nearest(k)
        for a in range(2):
            if stage > 0:
                for mask in fresh_masks(a, stage - 1):
                    arrived(core, a, zz, mirror(mask))
            for mask in mask_list(a, stage):
                send(
                    core, a, zz, mirror(mask), esem, peer(z, core, mirror(bit_of(a, stage)))
                ).start()
            if stage > 0:
                for mask in fresh_masks(a, stage - 1):
                    to_sibling(a, zz, mirror(mask))

    def last_arrivals(k):
        zz = nearest(k)
        for a in range(2):
            for mask in fresh_masks(a, stages - 1):
                arrived(core, a, zz, mirror(mask))
                to_sibling(a, zz, mirror(mask))

    contract_last = (((1,), (1,)), ((), ()))

    def compute(k):
        zz = nearest(k)
        for turn in range(2):
            c = core if turn == 0 else other
            if turn == 1:
                for a in range(2):
                    for mask in range(groups):
                        arrived(c, a, zz, mirror(mask))
            f = zz * CORES + c
            columns = pl.ds(pl.multiple_of(f * features, features), features)
            x = buf[c, 0, zz].reshape(groups * tokens_each, features)
            y = buf[c, 1, zz].reshape(groups * tokens_each, features)
            for e in range(local):
                chosen = jnp.dot(
                    sel[e], x, preferred_element_type=jnp.float32
                ).astype(jnp.bfloat16)
                scaled = (
                    jnp.dot(sel[e], y, preferred_element_type=jnp.float32) * gsel[e][:, :1]
                ).astype(jnp.bfloat16)
                rows[f, 0, e] = chosen
                rows[f, 1, e] = scaled
                for part, right in enumerate((chosen, chosen, scaled)):
                    acc[e, part] += lax.dot_general(
                        wbuf[e, part, :, columns], right, contract_last,
                        preferred_element_type=jnp.float32,
                    )
            pltpu.make_async_copy(rows.at[f], rows_ref.at[f], rowsem).start()

    for mask in range(1, groups):
        pltpu.make_async_remote_copy(
            src_ref=metab.at[own], dst_ref=metab.at[own], send_sem=msem_s,
            recv_sem=msem_r.at[own], device_id=peer(z, core, mirror(mask)),
            device_id_type=MESH,
        ).start()
    stage_send(0, 0)
    z_forward(z, True)
    for e in range(local):
        pltpu.make_async_copy(w_ref.at[e], wbuf.at[e], wsem).start()

    acc[...] = jnp.zeros_like(acc)
    for mask in range(1, groups):
        s = mirror(mask)
        pltpu.make_async_copy(metab.at[s], metab.at[s], msem_r.at[s]).wait()
    triangle = (
        lax.broadcasted_iota(jnp.int32, (tokens_each, tokens_each), 0)
        < lax.broadcasted_iota(jnp.int32, (tokens_each, tokens_each), 1)
    ).astype(jnp.bfloat16)
    slots = lax.broadcasted_iota(jnp.int32, (length, tokens_each), 0).astype(jnp.float32)
    for e in range(local):
        wanted = (own * local + e).astype(jnp.float32)
        opening = jnp.zeros((1, 1), jnp.float32)
        gate_sum = jnp.zeros((length, 1), jnp.float32)
        for s in range(groups):
            table = metab[s]
            hit = jnp.zeros((1, tokens_each), jnp.float32)
            gate = jnp.zeros((1, tokens_each), jnp.float32)
            for k in range(per_token):
                same = table[k:k + 1] == wanted
                hit = jnp.where(same, 1.0, hit)
                gate = jnp.where(same, table[per_token + k:per_token + k + 1], gate)
            wide = jnp.broadcast_to(hit, (16, tokens_each)).astype(jnp.bfloat16)
            place = jnp.dot(wide, triangle, preferred_element_type=jnp.float32)[:1] + opening
            opening = opening + jnp.sum(hit, axis=1, keepdims=True)
            picked = (slots == place) & (hit > 0.5)
            sel[e, :, s * tokens_each:(s + 1) * tokens_each] = jnp.where(
                picked, 1.0, 0.0
            ).astype(jnp.bfloat16)
            gate_sum = gate_sum + jnp.sum(
                jnp.where(picked, gate, 0.0), axis=1, keepdims=True
            )
        gsel[e] = jnp.broadcast_to(gate_sum, gsel.shape[1:])

    def step(k, carry):
        @pl.when((k > 0) & (k < chips))
        def _():
            @pl.when(z - k >= 0)
            def _():
                z_forward(z - k, False)

            @pl.when(z + k < chips)
            def _():
                z_forward(z + k, False)

            stage_send(k, 0)

        for stage in range(1, stages):
            @pl.when((k >= stage) & (k < chips + stage))
            def _(stage=stage):
                stage_send(k - stage, stage)

        @pl.when((k >= stages) & (k < chips + stages))
        def _():
            last_arrivals(k - stages)

        @pl.when(k == stages + 1)
        def _():
            pltpu.make_async_copy(w_ref, wbuf, wsem).wait()

        @pl.when(k >= stages + 1)
        def _():
            compute(k - stages - 1)

        return carry

    lax.fori_loop(0, chips + stages + 1, step, 0)

    for e in range(local):
        gate_part, up_part, back = acc[e, 0], acc[e, 1], acc[e, 2]
        sigmoid = jax.nn.sigmoid(gate_part)
        silu = gate_part * sigmoid
        pre_ref[e, 0] = (
            back * up_part * (sigmoid * (1.0 + gate_part * (1.0 - sigmoid)))
        ).astype(jnp.bfloat16)
        pre_ref[e, 1] = (back * silu).astype(jnp.bfloat16)
        pre_ref[e, 2] = (silu * up_part).astype(jnp.bfloat16)

    def z_drain(zz, carry):
        for a in range(2):
            @pl.when((zz <= z) & (z < chips - 1))
            def _():
                z_send(zz, a, True).wait_send()

            @pl.when((zz >= z) & (z > 0))
            def _():
                z_send(zz, a, False).wait_send()

        return carry

    lax.fori_loop(0, chips, z_drain, 0)
    sent = buf.at[0, :, :, pl.ds(0, groups - 1)]
    pltpu.make_async_copy(sent, sent, esem).wait()
    pltpu.make_async_copy(buf.at[0], buf.at[0], bsem).wait()
    sent = metab.at[pl.ds(0, groups - 1)]
    pltpu.make_async_copy(sent, sent, msem_s).wait()
    pltpu.make_async_copy(rows, rows_ref, rowsem).wait()


def outer_kernel(pre_ref, rows_ref, out_ref):
    pieces, features = rows_ref.shape[0], rows_ref.shape[-1]
    for piece in range(pieces):
        columns = slice(piece * features, (piece + 1) * features)
        for part, which in enumerate((0, 0, 1)):
            out_ref[0, part, :, columns] = jnp.dot(
                pre_ref[0, part], rows_ref[piece, which, 0],
                preferred_element_type=jnp.float32,
            ).astype(jnp.bfloat16)


def per_device(tokens, cotangent, routes, gates, expert_weights):
    local, parts, hidden, total_features = expert_weights.shape
    tokens_each, features = tokens.shape
    per_token = routes.shape[1]
    groups = lax.axis_size("expert")
    devices = lax.axis_size("dp")
    chips = devices // CORES
    length = groups * CAP
    meta = jnp.concatenate([routes.astype(jnp.float32), gates], axis=1).T
    meta_rows = -(-meta.shape[0] // 8) * 8
    meta = jnp.pad(meta, ((0, meta_rows - meta.shape[0]), (0, 0)))
    sizes = (chips, groups, local, per_token, length)
    any_space = pl.BlockSpec(memory_space=pl.ANY)
    rows, pre = pl.pallas_call(
        functools.partial(exchange_kernel, sizes),
        out_shape=(
            jax.ShapeDtypeStruct((devices, 2, local, length, features), jnp.bfloat16),
            jax.ShapeDtypeStruct((local, parts, hidden, length), jnp.bfloat16),
        ),
        in_specs=[any_space] * 4,
        out_specs=(any_space, pl.BlockSpec(memory_space=pltpu.VMEM)),
        scratch_shapes=[
            pltpu.VMEM((CORES, 2, chips, groups, tokens_each, features), jnp.bfloat16),
            pltpu.VMEM((groups, meta_rows, tokens_each), jnp.float32),
            pltpu.VMEM(expert_weights.shape, jnp.bfloat16),
            pltpu.VMEM((local, length, groups * tokens_each), jnp.bfloat16),
            pltpu.VMEM((local, length, 128), jnp.float32),
            pltpu.VMEM((devices, 2, local, length, features), jnp.bfloat16),
            pltpu.VMEM((local, parts, hidden, length), jnp.float32),
            pltpu.SemaphoreType.DMA((CORES, 2, chips, groups)),
            pltpu.SemaphoreType.DMA((2, chips, 2)),
            pltpu.SemaphoreType.DMA,
            pltpu.SemaphoreType.DMA,
            pltpu.SemaphoreType.DMA((groups,)),
            pltpu.SemaphoreType.DMA,
            pltpu.SemaphoreType.DMA((3,)),
            pltpu.SemaphoreType.DMA,
            pltpu.SemaphoreType.DMA,
        ],
        compiler_params=pltpu.CompilerParams(
            collective_id=0, has_side_effects=True, vmem_limit_bytes=60 * 1024 * 1024
        ),
        name="exchange",
    )(tokens, cotangent, meta, expert_weights)
    pieces = max(1, devices // 4)
    return pl.pallas_call(
        outer_kernel,
        out_shape=jax.ShapeDtypeStruct(expert_weights.shape, jnp.bfloat16),
        grid=(local, devices // pieces),
        in_specs=[
            pl.BlockSpec((1, parts, hidden, length), lambda e, j: (e, 0, 0, 0)),
            pl.BlockSpec((pieces, 2, 1, length, features), lambda e, j: (j, 0, e, 0, 0)),
        ],
        out_specs=pl.BlockSpec(
            (1, parts, hidden, pieces * features), lambda e, j: (e, 0, 0, j)
        ),
        compiler_params=pltpu.CompilerParams(vmem_limit_bytes=48 * 1024 * 1024),
        name="outer",
    )(pre, rows)


def solution(mesh):
    return jax.shard_map(
        per_device,
        mesh=mesh,
        in_specs=(
            P("expert", "dp"),
            P("expert", "dp"),
            P("expert", None),
            P("expert", None),
            P("expert", None, "dp", None),
        ),
        out_specs=P("expert", None, "dp", None),
        check_vma=False,
    )
```

time: 406 us -> 77.5 us (0.19)
  the two profiles are of different devices: /device:TPU:5 before, /device:TPU:0 now
where the time goes in v1:
time: 77.5 us; the launch traced here: 76.9 us
  Pallas kernels  73.5 us (95%)
  local copies, waits for them, and re-layouts  2 us (3%)
  other arithmetic  1.37 us (2%)
    pallas_call x1, Pallas kernels, per_device(): pl.pallas_call(functools.partial(exchange_kernel, sizes), out_shape=(jax....  54.2 us
    pallas_call x1, Pallas kernels, per_device(): pl.pallas_call(outer_kernel, out_shape=jax.ShapeDtypeStruct(expert_weight...  19.3 us

profile of v1, /device:TPU:0, one launch (start us, length us, event | category | flops | bytes accessed | tf_op | source)
XLA Modules:
  0.0 76.9 jit_solution(1417929300076053949)
XLA Ops:
  0.0 0.7 convert_element_type.5
  0.7 0.7 maximum_bitcast_fusion
  1.4 0.6 pad.4.meta_ref
  2.0 54.2 %exchange.1 = (bf16[8,2,4,160,512]{4,3,2,1,0:T(8,128)(2,1)}, bf16[4,3,256,160]{3,2,1,0:T(8,128)(2,1)}) custom-call(bf16[128,512]{1,0:T(8,128)(2,1)} %tok_ref.1, bf16[128,512]{1,0:T(8,128)(2,1)} %cot_ref.1, f32[8,128]{1,0:T(8,128)} %pad.4.meta_ref, bf16[4,3,256,4096]{3,2,1,0:T(8,128)(2,1)} %w_ref.1), custom_call_target="tpu_custom_call" | custom-call | tf_op jit(solution)/shard_map/exchange/pallas_call | solution.py:299
  56.2 0.0 copy-start
  56.2 1.4 %copy-done = bf16[4,3,256,160]{3,2,1,0:T(8,128)(2,1)S(1)} copy-done((bf16[4,3,256,160]{3,2,1,0:T(8,128)(2,1)S(1)}, bf16[4,3,256,160]{3,2,1,0:T(8,128)(2,1)}, u32[]{:S(2)}) %copy-start) | copy-done | bytes 983064
  57.6 19.3 %outer.1 = bf16[4,3,256,4096]{3,2,1,0:T(8,128)(2,1)} custom-call(bf16[4,3,256,160]{3,2,1,0:T(8,128)(2,1)S(1)} %copy-done, bf16[8,2,4,160,512]{4,3,2,1,0:T(8,128)(2,1)} %get-tuple-element.8.rows_ref), custom_call_target="tpu_custom_call" | custom-call | tf_op jit(solution)/shard_map/outer/pallas_call | solution.py:331
Async XLA Ops:
  56.2 1.4 %copy-start = (bf16[4,3,256,160]{3,2,1,0:T(8,128)(2,1)S(1)}, bf16[4,3,256,160]{3,2,1,0:T(8,128)(2,1)}, u32[]{:S(2)}) copy-start(bf16[4,3,256,160]{3,2,1,0:T(8,128)(2,1)} %get-tuple-element.7.pre_ref) | copy-start | bytes 2949124

commit v2 on v1

--- a/solution.py
+++ b/solution.py
@@ -13,7 +13,7 @@
 
 
 def exchange_kernel(
-    sizes, tok_ref, cot_ref, meta_ref, w_ref,
+    sizes, tok_ref, cot_ref, routes_ref, gates_ref, w_ref,
     rows_ref, pre_ref,
     buf, metab, wbuf, sel, gsel, rows, acc,
     rsem, zsem, esem, bsem, msem_r, msem_s, osem, wsem, rowsem,
@@ -25,6 +25,7 @@
     z, core = dp // CORES, dp % CORES
     other = 1 - core
     tokens_each, features = tok_ref.shape
+    hidden = w_ref.shape[2]
 
     def peer(z_to, core_to, group_to):
         return (z_to * CORES + core_to, group_to)
@@ -42,9 +43,12 @@
     own_copies = [
         pltpu.make_async_copy(ref, buf.at[core, a, z, own], osem.at[a])
         for a, ref in enumerate((tok_ref, cot_ref))
-    ] + [pltpu.make_async_copy(meta_ref, metab.at[own], osem.at[2])]
+    ]
     for copy in own_copies:
         copy.start()
+    metab[own] = jnp.zeros(metab.shape[1:], jnp.float32)
+    metab[own, 0:per_token] = routes_ref[...].astype(jnp.float32)
+    metab[own, per_token:2 * per_token] = gates_ref[...]
 
     greeted = [
         peer(lax.rem(z + 1, chips), core, own),
@@ -147,20 +151,24 @@
             columns = pl.ds(pl.multiple_of(f * features, features), features)
             x = buf[c, 0, zz].reshape(groups * tokens_each, features)
             y = buf[c, 1, zz].reshape(groups * tokens_each, features)
+            pick = sel[...].reshape(local * length, groups * tokens_each)
+            rows[f, 0] = (
+                jnp.dot(pick, x, preferred_element_type=jnp.float32)
+                .astype(jnp.bfloat16).reshape(local, length, features)
+            )
+            rows[f, 1] = (
+                (jnp.dot(pick, y, preferred_element_type=jnp.float32) * gsel[:, :1])
+                .astype(jnp.bfloat16).reshape(local, length, features)
+            )
             for e in range(local):
-                chosen = jnp.dot(
-                    sel[e], x, preferred_element_type=jnp.float32
-                ).astype(jnp.bfloat16)
-                scaled = (
-                    jnp.dot(sel[e], y, preferred_element_type=jnp.float32) * gsel[e][:, :1]
-                ).astype(jnp.bfloat16)
-                rows[f, 0, e] = chosen
-                rows[f, 1, e] = scaled
-                for part, right in enumerate((chosen, chosen, scaled)):
-                    acc[e, part] += lax.dot_general(
-                        wbuf[e, part, :, columns], right, contract_last,
-                        preferred_element_type=jnp.float32,
-                    )
+                acc[e, 0:2] += lax.dot_general(
+                    wbuf[e, 0:2, :, columns].reshape(2 * hidden, features), rows[f, 0, e],
+                    contract_last, preferred_element_type=jnp.float32,
+                ).reshape(2, hidden, length)
+                acc[e, 2] += lax.dot_general(
+                    wbuf[e, 2, :, columns], rows[f, 1, e],
+                    contract_last, preferred_element_type=jnp.float32,
+                )
             pltpu.make_async_copy(rows.at[f], rows_ref.at[f], rowsem).start()
 
     for mask in range(1, groups):
@@ -205,7 +213,7 @@
             gate_sum = gate_sum + jnp.sum(
                 jnp.where(picked, gate, 0.0), axis=1, keepdims=True
             )
-        gsel[e] = jnp.broadcast_to(gate_sum, gsel.shape[1:])
+        gsel[e * length:(e + 1) * length] = jnp.broadcast_to(gate_sum, (length, 128))
 
     def step(k, carry):
         @pl.when((k > 0) & (k < chips))
@@ -225,31 +233,35 @@
             def _(stage=stage):
                 stage_send(k - stage, stage)
 
+        @pl.when(k == stages + 1)
+        def _():
+            pltpu.make_async_copy(w_ref, wbuf, wsem).wait()
+
+        @pl.when(k >= stages + 1)
+        def _():
+            compute(k - stages - 1)
+
         @pl.when((k >= stages) & (k < chips + stages))
         def _():
             last_arrivals(k - stages)
 
-        @pl.when(k == stages + 1)
-        def _():
-            pltpu.make_async_copy(w_ref, wbuf, wsem).wait()
-
-        @pl.when(k >= stages + 1)
-        def _():
-            compute(k - stages - 1)
-
         return carry
 
     lax.fori_loop(0, chips + stages + 1, step, 0)
 
+    if pre_ref.shape[-1] > length:
+        pre_ref[:, :, :, length:] = jnp.zeros(
+            pre_ref.shape[:3] + (pre_ref.shape[-1] - length,), jnp.bfloat16
+        )
     for e in range(local):
         gate_part, up_part, back = acc[e, 0], acc[e, 1], acc[e, 2]
         sigmoid = jax.nn.sigmoid(gate_part)
         silu = gate_part * sigmoid
-        pre_ref[e, 0] = (
+        pre_ref[e, 0, :, :length] = (
             back * up_part * (sigmoid * (1.0 + gate_part * (1.0 - sigmoid)))
         ).astype(jnp.bfloat16)
-        pre_ref[e, 1] = (back * silu).astype(jnp.bfloat16)
-        pre_ref[e, 2] = (silu * up_part).astype(jnp.bfloat16)
+        pre_ref[e, 1, :, :length] = (back * silu).astype(jnp.bfloat16)
+        pre_ref[e, 2, :, :length] = (silu * up_part).astype(jnp.bfloat16)
 
     def z_drain(zz, carry):
         for a in range(2):
@@ -272,15 +284,68 @@
     pltpu.make_async_copy(rows, rows_ref, rowsem).wait()
 
 
-def outer_kernel(pre_ref, rows_ref, out_ref):
-    pieces, features = rows_ref.shape[0], rows_ref.shape[-1]
-    for piece in range(pieces):
-        columns = slice(piece * features, (piece + 1) * features)
-        for part, which in enumerate((0, 0, 1)):
-            out_ref[0, part, :, columns] = jnp.dot(
-                pre_ref[0, part], rows_ref[piece, which, 0],
+def outer_kernel(
+    pieces, length, pre_hbm, rows_ref, out_ref, pre, rbuf, obuf, insem, osem, psem
+):
+    local, parts, hidden, padded = pre.shape
+    devices, features = rbuf.shape[1], rbuf.shape[-1]
+    per_expert = devices // pieces
+    slots = obuf.shape[0]
+    steps = local * per_expert
+
+    def rows_in(e):
+        return pltpu.make_async_copy(
+            rows_ref.at[:, :, e], rbuf.at[e, :, :, pl.ds(0, length)], insem.at[e]
+        )
+
+    def write(step):
+        slot = step % slots
+        e, j = step // per_expert, step % per_expert
+        width = pieces * features
+        return pltpu.make_async_copy(
+            obuf.at[slot],
+            out_ref.at[e, :, :, pl.ds(pl.multiple_of(j * width, width), width)],
+            osem.at[slot],
+        )
+
+    pre_in = pltpu.make_async_copy(pre_hbm, pre, psem)
+    pre_in.start()
+    for e in range(local):
+        rows_in(e).start()
+    if padded > length:
+        rbuf[:, :, :, length:] = jnp.zeros(
+            rbuf.shape[:3] + (padded - length, features), jnp.bfloat16
+        )
+    pre_in.wait()
+
+    def one(step, carry):
+        slot = step % slots
+        e, j = step // per_expert, step % per_expert
+
+        @pl.when(j == 0)
+        def _():
+            rows_in(e).wait()
+
+        @pl.when(step >= slots)
+        def _():
+            write(step - slots).wait()
+
+        for piece in range(pieces):
+            f = j * pieces + piece
+            columns = slice(piece * features, (piece + 1) * features)
+            obuf[slot, 0:2, :, columns] = jnp.dot(
+                pre[e, 0:2].reshape(2 * hidden, padded), rbuf[e, f, 0],
                 preferred_element_type=jnp.float32,
+            ).astype(jnp.bfloat16).reshape(2, hidden, features)
+            obuf[slot, 2, :, columns] = jnp.dot(
+                pre[e, 2], rbuf[e, f, 1], preferred_element_type=jnp.float32
             ).astype(jnp.bfloat16)
+        write(step).start()
+        return carry
+
+    lax.fori_loop(0, steps, one, 0)
+    for step in range(max(0, steps - slots), steps):
+        write(step).wait()
 
 
 def per_device(tokens, cotangent, routes, gates, expert_weights):
@@ -291,25 +356,25 @@
     devices = lax.axis_size("dp")
     chips = devices // CORES
     length = groups * CAP
-    meta = jnp.concatenate([routes.astype(jnp.float32), gates], axis=1).T
-    meta_rows = -(-meta.shape[0] // 8) * 8
-    meta = jnp.pad(meta, ((0, meta_rows - meta.shape[0]), (0, 0)))
+    meta_rows = -(-2 * per_token // 8) * 8
+    padded = -(-length // 128) * 128
     sizes = (chips, groups, local, per_token, length)
     any_space = pl.BlockSpec(memory_space=pl.ANY)
+    in_vmem = pl.BlockSpec(memory_space=pltpu.VMEM)
     rows, pre = pl.pallas_call(
         functools.partial(exchange_kernel, sizes),
         out_shape=(
             jax.ShapeDtypeStruct((devices, 2, local, length, features), jnp.bfloat16),
-            jax.ShapeDtypeStruct((local, parts, hidden, length), jnp.bfloat16),
+            jax.ShapeDtypeStruct((local, parts, hidden, padded), jnp.bfloat16),
         ),
-        in_specs=[any_space] * 4,
-        out_specs=(any_space, pl.BlockSpec(memory_space=pltpu.VMEM)),
+        in_specs=[any_space, any_space, in_vmem, in_vmem, any_space],
+        out_specs=(any_space, in_vmem),
         scratch_shapes=[
             pltpu.VMEM((CORES, 2, chips, groups, tokens_each, features), jnp.bfloat16),
             pltpu.VMEM((groups, meta_rows, tokens_each), jnp.float32),
             pltpu.VMEM(expert_weights.shape, jnp.bfloat16),
             pltpu.VMEM((local, length, groups * tokens_each), jnp.bfloat16),
-            pltpu.VMEM((local, length, 128), jnp.float32),
+            pltpu.VMEM((local * length, 128), jnp.float32),
             pltpu.VMEM((devices, 2, local, length, features), jnp.bfloat16),
             pltpu.VMEM((local, parts, hidden, length), jnp.float32),
             pltpu.SemaphoreType.DMA((CORES, 2, chips, groups)),
@@ -318,7 +383,7 @@
             pltpu.SemaphoreType.DMA,
             pltpu.SemaphoreType.DMA((groups,)),
             pltpu.SemaphoreType.DMA,
-            pltpu.SemaphoreType.DMA((3,)),
+            pltpu.SemaphoreType.DMA((2,)),
             pltpu.SemaphoreType.DMA,
             pltpu.SemaphoreType.DMA,
         ],
@@ -326,20 +391,23 @@
             collective_id=0, has_side_effects=True, vmem_limit_bytes=60 * 1024 * 1024
         ),
         name="exchange",
-    )(tokens, cotangent, meta, expert_weights)
+    )(tokens, cotangent, routes.T, gates.T, expert_weights)
     pieces = max(1, devices // 4)
+    slots = 5
     return pl.pallas_call(
-        outer_kernel,
+        functools.partial(outer_kernel, pieces, length),
         out_shape=jax.ShapeDtypeStruct(expert_weights.shape, jnp.bfloat16),
-        grid=(local, devices // pieces),
-        in_specs=[
-            pl.BlockSpec((1, parts, hidden, length), lambda e, j: (e, 0, 0, 0)),
-            pl.BlockSpec((pieces, 2, 1, length, features), lambda e, j: (j, 0, e, 0, 0)),
+        in_specs=[any_space] * 2,
+        out_specs=any_space,
+        scratch_shapes=[
+            pltpu.VMEM((local, parts, hidden, padded), jnp.bfloat16),
+            pltpu.VMEM((local, devices, 2, padded, features), jnp.bfloat16),
+            pltpu.VMEM((slots, parts, hidden, pieces * features), jnp.bfloat16),
+            pltpu.SemaphoreType.DMA((local,)),
+            pltpu.SemaphoreType.DMA((slots,)),
+            pltpu.SemaphoreType.DMA,
         ],
-        out_specs=pl.BlockSpec(
-            (1, parts, hidden, pieces * features), lambda e, j: (e, 0, 0, j)
-        ),
-        compiler_params=pltpu.CompilerParams(vmem_limit_bytes=48 * 1024 * 1024),
+        compiler_params=pltpu.CompilerParams(vmem_limit_bytes=60 * 1024 * 1024),
         name="outer",
     )(pre, rows)
 

time: 77.5 us -> 65.6 us (0.85)
  Pallas kernels: 73.5 us -> 65.4 us
  local copies, waits for them, and re-layouts: 2 us -> 0 us
  other arithmetic: 1.37 us -> 0 us
    pallas_call x1, Pallas kernels: 19.3 us -> 15.1 us  [per_device(): pl.pallas_call(functools.partial(outer_kernel, pieces, length), out_shape...]
    pallas_call x1, Pallas kernels: 54.2 us -> 50.2 us  [per_device(): pl.pallas_call(functools.partial(exchange_kernel, sizes), out_shape=(jax....]
    unnamed x2 -> x0, local copies, waits for them, and re-layouts: 1.4 us -> none
where the time goes in v2:
time: 65.6 us; the launch traced here: 65.4 us
  Pallas kernels  65.4 us (100%)
    pallas_call x1, Pallas kernels, per_device(): pl.pallas_call(functools.partial(exchange_kernel, sizes), out_shape=(jax....  50.2 us
    pallas_call x1, Pallas kernels, per_device(): pl.pallas_call(functools.partial(outer_kernel, pieces, length), out_shape...  15.1 us

profile of v2, /device:TPU:0, one launch (start us, length us, event | category | flops | bytes accessed | tf_op | source)
XLA Modules:
  0.0 65.4 jit_solution(8059452033150017418)
XLA Ops:
  0.0 50.2 %exchange.1 = (bf16[8,2,4,160,512]{4,3,2,1,0:T(8,128)(2,1)}, bf16[4,3,256,256]{3,2,1,0:T(8,128)(2,1)}) custom-call(bf16[128,512]{1,0:T(8,128)(2,1)} %tok_ref.1, bf16[128,512]{1,0:T(8,128)(2,1)} %cot_ref.1, s32[2,128]{1,0:T(2,128)} %bitcast.2, f32[2,128]{1,0:T(2,128)} %bitcast.3, bf16[4,3,256,4096]{3,2,1,0:T(8,128)(2,1)} %w_ref.1), custom_call_target="tpu_custom_call" | custom-call | tf_op jit(solution)/shard_map/exchange/pallas_call | solution.py:364
  50.2 15.1 %outer.1 = bf16[4,3,256,4096]{3,2,1,0:T(8,128)(2,1)} custom-call(bf16[4,3,256,256]{3,2,1,0:T(8,128)(2,1)} %get-tuple-element.7.pre_hbm, bf16[8,2,4,160,512]{4,3,2,1,0:T(8,128)(2,1)} %get-tuple-element.8.rows_ref), custom_call_target="tpu_custom_call" | custom-call | tf_op jit(solution)/shard_map/outer/pallas_call | solution.py:397

commit v3 on v2

--- a/solution.py
+++ b/solution.py
@@ -9,6 +9,7 @@
 
 CAP = 40
 CORES = 2
+REACH = 2
 MESH = pl.DeviceIdType.MESH
 
 
@@ -16,7 +17,7 @@
     sizes, tok_ref, cot_ref, routes_ref, gates_ref, w_ref,
     rows_ref, pre_ref,
     buf, metab, wbuf, sel, gsel, rows, acc,
-    rsem, zsem, esem, bsem, msem_r, msem_s, osem, wsem, rowsem,
+    rsem, zsem, farsem, diagsem, esem, bsem, msem_r, msem_s, osem, wsem, rowsem,
 ):
     chips, groups, local, per_token, length = sizes
     stages = groups.bit_length() - 1
@@ -95,10 +96,45 @@
         rest = jnp.where(2 * z < chips, k, chips - 1 - k)
         return jnp.where(k <= 2 * m, side, rest)
 
-    def z_send(zz, a, upward):
+    def z_send(zz, a, upward, s=own, sem=zsem):
         return send(
-            core, a, zz, own, zsem.at[a, zz, 0 if upward else 1],
+            core, a, zz, s, sem.at[a, zz, 0 if upward else 1],
             peer(z + 1 if upward else z - 1, core, own),
+        )
+
+    far = groups - 1
+    by_z = stages > 1
+
+    def over_z(zz):
+        return (zz != z) & (zz - z <= REACH) & (z - zz <= REACH)
+
+    def far_up(zz):
+        return (zz <= z) & (z < chips - 1) & (z + 1 - zz <= REACH)
+
+    def far_down(zz):
+        return (zz >= z) & (z > 0) & (zz - z + 1 <= REACH)
+
+    def far_forward(zz, first):
+        s = mirror(far)
+        for a in range(2):
+            if not first:
+                arrived(core, a, zz, s)
+
+            @pl.when(far_up(zz))
+            def _():
+                z_send(zz, a, True, s, farsem).start()
+
+            @pl.when(far_down(zz))
+            def _():
+                z_send(zz, a, False, s, farsem).start()
+
+            if not first:
+                to_sibling(a, zz, s)
+
+    def far_send(zz, a):
+        bit = bit_of(a, stages - 1)
+        return send(
+            core, a, zz, mirror(far ^ bit), diagsem.at[a, zz], peer(z, core, mirror(bit))
         )
 
     def z_forward(zz, first):
@@ -123,6 +159,11 @@
                 for mask in fresh_masks(a, stage - 1):
                     arrived(core, a, zz, mirror(mask))
             for mask in mask_list(a, stage):
+                if by_z and stage == stages - 1 and mask == far ^ bit_of(a, stage):
+                    @pl.when(jnp.logical_not(over_z(zz)))
+                    def _():
+                        far_send(zz, a).start()
+                    continue
                 send(
                     core, a, zz, mirror(mask), esem, peer(z, core, mirror(bit_of(a, stage)))
                 ).start()
@@ -134,6 +175,12 @@
         zz = nearest(k)
         for a in range(2):
             for mask in fresh_masks(a, stages - 1):
+                if by_z and mask == far:
+                    @pl.when(jnp.logical_not(over_z(zz)))
+                    def _():
+                        arrived(core, a, zz, mirror(far))
+                        to_sibling(a, zz, mirror(far))
+                    continue
                 arrived(core, a, zz, mirror(mask))
                 to_sibling(a, zz, mirror(mask))
 
@@ -233,6 +280,19 @@
             def _(stage=stage):
                 stage_send(k - stage, stage)
 
+        if by_z:
+            distance = k - stages
+
+            @pl.when((distance > 0) & (distance <= REACH))
+            def _():
+                @pl.when(z - distance >= 0)
+                def _():
+                    far_forward(z - distance, False)
+
+                @pl.when(z + distance < chips)
+                def _():
+                    far_forward(z + distance, False)
+
         @pl.when(k == stages + 1)
         def _():
             pltpu.make_async_copy(w_ref, wbuf, wsem).wait()
@@ -244,6 +304,11 @@
         @pl.when((k >= stages) & (k < chips + stages))
         def _():
             last_arrivals(k - stages)
+
+        if by_z:
+            @pl.when(k == stages)
+            def _():
+                far_forward(z, True)
 
         return carry
 
@@ -273,10 +338,23 @@
             def _():
                 z_send(zz, a, False).wait_send()
 
+            if by_z:
+                @pl.when(far_up(zz))
+                def _():
+                    z_send(zz, a, True, mirror(far), farsem).wait_send()
+
+                @pl.when(far_down(zz))
+                def _():
+                    z_send(zz, a, False, mirror(far), farsem).wait_send()
+
+                @pl.when(jnp.logical_not(over_z(zz)))
+                def _():
+                    far_send(zz, a).wait_send()
+
         return carry
 
     lax.fori_loop(0, chips, z_drain, 0)
-    sent = buf.at[0, :, :, pl.ds(0, groups - 1)]
+    sent = buf.at[0, :, :, pl.ds(0, groups - 2 if by_z else groups - 1)]
     pltpu.make_async_copy(sent, sent, esem).wait()
     pltpu.make_async_copy(buf.at[0], buf.at[0], bsem).wait()
     sent = metab.at[pl.ds(0, groups - 1)]
@@ -379,6 +457,8 @@
             pltpu.VMEM((local, parts, hidden, length), jnp.float32),
             pltpu.SemaphoreType.DMA((CORES, 2, chips, groups)),
             pltpu.SemaphoreType.DMA((2, chips, 2)),
+            pltpu.SemaphoreType.DMA((2, chips, 2)),
+            pltpu.SemaphoreType.DMA((2, chips)),
             pltpu.SemaphoreType.DMA,
             pltpu.SemaphoreType.DMA,
             pltpu.SemaphoreType.DMA((groups,)),

time: 65.6 us -> 64.7 us (0.986)
  Pallas kernels: 65.4 us -> 64.5 us
    pallas_call x1, Pallas kernels: 50.2 us -> 49.4 us  [per_device(): pl.pallas_call(functools.partial(exchange_kernel, sizes), out_shape=(jax....]
where the time goes in v3:
time: 64.7 us; the launch traced here: 64.6 us
  Pallas kernels  64.5 us (100%)
    pallas_call x1, Pallas kernels, per_device(): pl.pallas_call(functools.partial(exchange_kernel, sizes), out_shape=(jax....  49.4 us
    pallas_call x1, Pallas kernels, per_device(): pl.pallas_call(functools.partial(outer_kernel, pieces, length), out_shape...  15.1 us

profile of v3, /device:TPU:0, one launch (start us, length us, event | category | flops | bytes accessed | tf_op | source)
XLA Modules:
  0.0 64.6 jit_solution(17995553233118580087)
XLA Ops:
  0.0 49.4 %exchange.1 = (bf16[8,2,4,160,512]{4,3,2,1,0:T(8,128)(2,1)}, bf16[4,3,256,256]{3,2,1,0:T(8,128)(2,1)}) custom-call(bf16[128,512]{1,0:T(8,128)(2,1)} %tok_ref.1, bf16[128,512]{1,0:T(8,128)(2,1)} %cot_ref.1, s32[2,128]{1,0:T(2,128)} %bitcast.2, f32[2,128]{1,0:T(2,128)} %bitcast.3, bf16[4,3,256,4096]{3,2,1,0:T(8,128)(2,1)} %w_ref.1), custom_call_target="tpu_custom_call" | custom-call | tf_op jit(solution)/shard_map/exchange/pallas_call | solution.py:442
  49.4 15.1 %outer.1 = bf16[4,3,256,4096]{3,2,1,0:T(8,128)(2,1)} custom-call(bf16[4,3,256,256]{3,2,1,0:T(8,128)(2,1)} %get-tuple-element.7.pre_hbm, bf16[8,2,4,160,512]{4,3,2,1,0:T(8,128)(2,1)} %get-tuple-element.8.rows_ref), custom_call_target="tpu_custom_call" | custom-call | tf_op jit(solution)/shard_map/outer/pallas_call | solution.py:477

commit v4 on v3

--- a/solution.py
+++ b/solution.py
@@ -263,6 +263,14 @@
         gsel[e * length:(e + 1) * length] = jnp.broadcast_to(gate_sum, (length, 128))
 
     def step(k, carry):
+        @pl.when(k == stages + 1)
+        def _():
+            pltpu.make_async_copy(w_ref, wbuf, wsem).wait()
+
+        @pl.when(k >= stages + 1)
+        def _():
+            compute(k - stages - 1)
+
         @pl.when((k > 0) & (k < chips))
         def _():
             @pl.when(z - k >= 0)
@@ -292,14 +300,6 @@
                 @pl.when(z + distance < chips)
                 def _():
                     far_forward(z + distance, False)
-
-        @pl.when(k == stages + 1)
-        def _():
-            pltpu.make_async_copy(w_ref, wbuf, wsem).wait()
-
-        @pl.when(k >= stages + 1)
-        def _():
-            compute(k - stages - 1)
 
         @pl.when((k >= stages) & (k < chips + stages))
         def _():
@@ -371,10 +371,15 @@
     slots = obuf.shape[0]
     steps = local * per_expert
 
-    def rows_in(e):
+    def rows_in(step):
+        e, first = step // per_expert, step % per_expert * pieces
         return pltpu.make_async_copy(
-            rows_ref.at[:, :, e], rbuf.at[e, :, :, pl.ds(0, length)], insem.at[e]
-        )
+            rows_ref.at[pl.ds(first, pieces), :, e],
+            rbuf.at[e, pl.ds(first, pieces), :, pl.ds(0, length)], insem.at[step],
+        )
+
+    def pre_in(e):
+        return pltpu.make_async_copy(pre_hbm.at[e], pre.at[e], psem.at[e])
 
     def write(step):
         slot = step % slots
@@ -386,23 +391,29 @@
             osem.at[slot],
         )
 
-    pre_in = pltpu.make_async_copy(pre_hbm, pre, psem)
-    pre_in.start()
-    for e in range(local):
-        rows_in(e).start()
+    pre_in(0).start()
+    ahead = min(4, steps)
+    for step in range(ahead):
+        rows_in(step).start()
+    for e in range(1, local):
+        pre_in(e).start()
     if padded > length:
         rbuf[:, :, :, length:] = jnp.zeros(
             rbuf.shape[:3] + (padded - length, features), jnp.bfloat16
         )
-    pre_in.wait()
-
     def one(step, carry):
         slot = step % slots
         e, j = step // per_expert, step % per_expert
 
         @pl.when(j == 0)
         def _():
-            rows_in(e).wait()
+            pre_in(e).wait()
+
+        rows_in(step).wait()
+
+        @pl.when(step + ahead < steps)
+        def _():
+            rows_in(step + ahead).start()
 
         @pl.when(step >= slots)
         def _():
@@ -483,9 +494,9 @@
             pltpu.VMEM((local, parts, hidden, padded), jnp.bfloat16),
             pltpu.VMEM((local, devices, 2, padded, features), jnp.bfloat16),
             pltpu.VMEM((slots, parts, hidden, pieces * features), jnp.bfloat16),
+            pltpu.SemaphoreType.DMA((local * (devices // pieces),)),
+            pltpu.SemaphoreType.DMA((slots,)),
             pltpu.SemaphoreType.DMA((local,)),
-            pltpu.SemaphoreType.DMA((slots,)),
-            pltpu.SemaphoreType.DMA,
         ],
         compiler_params=pltpu.CompilerParams(vmem_limit_bytes=60 * 1024 * 1024),
         name="outer",

time: 64.7 us -> 61.8 us (0.955)
  Pallas kernels: 64.5 us -> 61.6 us
    pallas_call x1, Pallas kernels: 15.1 us -> 12.4 us  [per_device(): pl.pallas_call(functools.partial(outer_kernel, pieces, length), out_shape...]
where the time goes in v4:
time: 61.8 us; the launch traced here: 61.6 us
  Pallas kernels  61.6 us (100%)
    pallas_call x1, Pallas kernels, per_device(): pl.pallas_call(functools.partial(exchange_kernel, sizes), out_shape=(jax....  49.2 us
    pallas_call x1, Pallas kernels, per_device(): pl.pallas_call(functools.partial(outer_kernel, pieces, length), out_shape...  12.4 us

profile of v4, /device:TPU:0, one launch (start us, length us, event | category | flops | bytes accessed | tf_op | source)
XLA Modules:
  0.0 61.6 jit_solution(7769400255264626501)
XLA Ops:
  0.0 49.2 %exchange.1 = (bf16[8,2,4,160,512]{4,3,2,1,0:T(8,128)(2,1)}, bf16[4,3,256,256]{3,2,1,0:T(8,128)(2,1)}) custom-call(bf16[128,512]{1,0:T(8,128)(2,1)} %tok_ref.1, bf16[128,512]{1,0:T(8,128)(2,1)} %cot_ref.1, s32[2,128]{1,0:T(2,128)} %bitcast.2, f32[2,128]{1,0:T(2,128)} %bitcast.3, bf16[4,3,256,4096]{3,2,1,0:T(8,128)(2,1)} %w_ref.1), custom_call_target="tpu_custom_call" | custom-call | tf_op jit(solution)/shard_map/exchange/pallas_call | solution.py:453
  49.2 12.4 %outer.1 = bf16[4,3,256,4096]{3,2,1,0:T(8,128)(2,1)} custom-call(bf16[4,3,256,256]{3,2,1,0:T(8,128)(2,1)} %get-tuple-element.7.pre_hbm, bf16[8,2,4,160,512]{4,3,2,1,0:T(8,128)(2,1)} %get-tuple-element.8.rows_ref), custom_call_target="tpu_custom_call" | custom-call | tf_op jit(solution)/shard_map/outer/pallas_call | solution.py:488

commit v5 on v4

--- a/solution.py
+++ b/solution.py
@@ -25,7 +25,10 @@
     own = lax.axis_index("expert")
     z, core = dp // CORES, dp % CORES
     other = 1 - core
-    tokens_each, features = tok_ref.shape
+    tokens_each = tok_ref.shape[0]
+    features = buf.shape[-1]
+    halves = tok_ref.shape[1] // features
+    count = chips * halves
     hidden = w_ref.shape[2]
 
     def peer(z_to, core_to, group_to):
@@ -42,8 +45,11 @@
         return result
 
     own_copies = [
-        pltpu.make_async_copy(ref, buf.at[core, a, z, own], osem.at[a])
-        for a, ref in enumerate((tok_ref, cot_ref))
+        pltpu.make_async_copy(
+            ref.at[:, half * features:(half + 1) * features],
+            buf.at[core, a, z * halves + half, own], osem.at[a, half],
+        )
+        for a, ref in enumerate((tok_ref, cot_ref)) for half in range(halves)
     ]
     for copy in own_copies:
         copy.start()
@@ -90,11 +96,12 @@
     def fresh_masks(a, stage):
         return [mask ^ bit_of(a, stage) for mask in mask_list(a, stage)]
 
-    def nearest(k):
+    def nearest(slot):
+        k = slot // halves
         m = jnp.where(2 * z < chips, z, chips - 1 - z)
         side = jnp.where(k % 2 == 1, z - (k + 1) // 2, z + k // 2)
         rest = jnp.where(2 * z < chips, k, chips - 1 - k)
-        return jnp.where(k <= 2 * m, side, rest)
+        return jnp.where(k <= 2 * m, side, rest) * halves + slot % halves
 
     def z_send(zz, a, upward, s=own, sem=zsem):
         return send(
@@ -105,18 +112,22 @@
     far = groups - 1
     by_z = stages > 1
 
-    def over_z(zz):
+    def over_z(block):
+        zz = block // halves
         return (zz != z) & (zz - z <= REACH) & (z - zz <= REACH)
 
-    def far_up(zz):
+    def far_up(block):
+        zz = block // halves
         return (zz <= z) & (z < chips - 1) & (z + 1 - zz <= REACH)
 
-    def far_down(zz):
+    def far_down(block):
+        zz = block // halves
         return (zz >= z) & (z > 0) & (zz - z + 1 <= REACH)
 
-    def far_forward(zz, first):
+    def far_forward(chip, first):
         s = mirror(far)
-        for a in range(2):
+        for half, a in halves_and_arrays:
+            zz = chip * halves + half
             if not first:
                 arrived(core, a, zz, s)
 
@@ -137,16 +148,25 @@
             core, a, zz, mirror(far ^ bit), diagsem.at[a, zz], peer(z, core, mirror(bit))
         )
 
-    def z_forward(zz, first):
-        for a in range(2):
+    halves_and_arrays = [(half, a) for half in range(halves) for a in range(2)]
+
+    def own_up(block):
+        return (block // halves <= z) & (z < chips - 1)
+
+    def own_down(block):
+        return (block // halves >= z) & (z > 0)
+
+    def z_forward(chip, first):
+        for half, a in halves_and_arrays:
+            zz = chip * halves + half
             if not first:
                 arrived(core, a, zz, own)
 
-            @pl.when((zz <= z) & (z < chips - 1))
+            @pl.when(own_up(zz))
             def _():
                 z_send(zz, a, True).start()
 
-            @pl.when((zz >= z) & (z > 0))
+            @pl.when(own_down(zz))
             def _():
                 z_send(zz, a, False).start()
 
@@ -194,7 +214,7 @@
                 for a in range(2):
                     for mask in range(groups):
                         arrived(c, a, zz, mirror(mask))
-            f = zz * CORES + c
+            f = (zz // halves * CORES + c) * halves + zz % halves
             columns = pl.ds(pl.multiple_of(f * features, features), features)
             x = buf[c, 0, zz].reshape(groups * tokens_each, features)
             y = buf[c, 1, zz].reshape(groups * tokens_each, features)
@@ -224,7 +244,8 @@
             recv_sem=msem_r.at[own], device_id=peer(z, core, mirror(mask)),
             device_id_type=MESH,
         ).start()
-    stage_send(0, 0)
+    for half in range(halves):
+        stage_send(half, 0)
     z_forward(z, True)
     for e in range(local):
         pltpu.make_async_copy(w_ref.at[e], wbuf.at[e], wsem).start()
@@ -271,48 +292,53 @@
         def _():
             compute(k - stages - 1)
 
-        @pl.when((k > 0) & (k < chips))
-        def _():
-            @pl.when(z - k >= 0)
-            def _():
-                z_forward(z - k, False)
-
-            @pl.when(z + k < chips)
-            def _():
-                z_forward(z + k, False)
-
-            stage_send(k, 0)
+        distance = k // halves
+
+        @pl.when((k > 0) & (k < count) & (k % halves == 0))
+        def _():
+            @pl.when(z - distance >= 0)
+            def _():
+                z_forward(z - distance, False)
+
+            @pl.when(z + distance < chips)
+            def _():
+                z_forward(z + distance, False)
+
+            for half in range(halves):
+                stage_send(k + half, 0)
 
         for stage in range(1, stages):
-            @pl.when((k >= stage) & (k < chips + stage))
+            @pl.when((k >= stage) & (k < count + stage))
             def _(stage=stage):
                 stage_send(k - stage, stage)
 
         if by_z:
-            distance = k - stages
-
-            @pl.when((distance > 0) & (distance <= REACH))
-            def _():
-                @pl.when(z - distance >= 0)
+            reach = (k - stages) // halves
+
+            @pl.when(
+                (k >= stages + halves) & (reach <= REACH) & ((k - stages) % halves == 0)
+            )
+            def _():
+                @pl.when(z - reach >= 0)
                 def _():
-                    far_forward(z - distance, False)
-
-                @pl.when(z + distance < chips)
+                    far_forward(z - reach, False)
+
+                @pl.when(z + reach < chips)
                 def _():
-                    far_forward(z + distance, False)
-
-        @pl.when((k >= stages) & (k < chips + stages))
+                    far_forward(z + reach, False)
+
+        @pl.when((k >= stages) & (k < count + stages))
         def _():
             last_arrivals(k - stages)
 
         if by_z:
-            @pl.when(k == stages)
+            @pl.when(k == stages + halves - 1)
             def _():
                 far_forward(z, True)
 
         return carry
 
-    lax.fori_loop(0, chips + stages + 1, step, 0)
+    lax.fori_loop(0, count + stages + 1, step, 0)
 
     if pre_ref.shape[-1] > length:
         pre_ref[:, :, :, length:] = jnp.zeros(
@@ -330,11 +356,11 @@
 
     def z_drain(zz, carry):
         for a in range(2):
-            @pl.when((zz <= z) & (z < chips - 1))
+            @pl.when(own_up(zz))
             def _():
                 z_send(zz, a, True).wait_send()
 
-            @pl.when((zz >= z) & (z > 0))
+            @pl.when(own_down(zz))
             def _():
                 z_send(zz, a, False).wait_send()
 
@@ -353,7 +379,7 @@
 
         return carry
 
-    lax.fori_loop(0, chips, z_drain, 0)
+    lax.fori_loop(0, count, z_drain, 0)
     sent = buf.at[0, :, :, pl.ds(0, groups - 2 if by_z else groups - 1)]
     pltpu.make_async_copy(sent, sent, esem).wait()
     pltpu.make_async_copy(buf.at[0], buf.at[0], bsem).wait()
@@ -447,34 +473,36 @@
     length = groups * CAP
     meta_rows = -(-2 * per_token // 8) * 8
     padded = -(-length // 128) * 128
+    halves = max(1, features // 256)
+    count, columns, blocks = chips * halves, features // halves, devices * halves
     sizes = (chips, groups, local, per_token, length)
     any_space = pl.BlockSpec(memory_space=pl.ANY)
     in_vmem = pl.BlockSpec(memory_space=pltpu.VMEM)
     rows, pre = pl.pallas_call(
         functools.partial(exchange_kernel, sizes),
         out_shape=(
-            jax.ShapeDtypeStruct((devices, 2, local, length, features), jnp.bfloat16),
+            jax.ShapeDtypeStruct((blocks, 2, local, length, columns), jnp.bfloat16),
             jax.ShapeDtypeStruct((local, parts, hidden, padded), jnp.bfloat16),
         ),
         in_specs=[any_space, any_space, in_vmem, in_vmem, any_space],
         out_specs=(any_space, in_vmem),
         scratch_shapes=[
-            pltpu.VMEM((CORES, 2, chips, groups, tokens_each, features), jnp.bfloat16),
+            pltpu.VMEM((CORES, 2, count, groups, tokens_each, columns), jnp.bfloat16),
             pltpu.VMEM((groups, meta_rows, tokens_each), jnp.float32),
             pltpu.VMEM(expert_weights.shape, jnp.bfloat16),
             pltpu.VMEM((local, length, groups * tokens_each), jnp.bfloat16),
             pltpu.VMEM((local * length, 128), jnp.float32),
-            pltpu.VMEM((devices, 2, local, length, features), jnp.bfloat16),
+            pltpu.VMEM((blocks, 2, local, length, columns), jnp.bfloat16),
             pltpu.VMEM((local, parts, hidden, length), jnp.float32),
-            pltpu.SemaphoreType.DMA((CORES, 2, chips, groups)),
-            pltpu.SemaphoreType.DMA((2, chips, 2)),
-            pltpu.SemaphoreType.DMA((2, chips, 2)),
-            pltpu.SemaphoreType.DMA((2, chips)),
+            pltpu.SemaphoreType.DMA((CORES, 2, count, groups)),
+            pltpu.SemaphoreType.DMA((2, count, 2)),
+            pltpu.SemaphoreType.DMA((2, count, 2)),
+            pltpu.SemaphoreType.DMA((2, count)),
             pltpu.SemaphoreType.DMA,
             pltpu.SemaphoreType.DMA,
             pltpu.SemaphoreType.DMA((groups,)),
             pltpu.SemaphoreType.DMA,
-            pltpu.SemaphoreType.DMA((2,)),
+            pltpu.SemaphoreType.DMA((2, halves)),
             pltpu.SemaphoreType.DMA,
             pltpu.SemaphoreType.DMA,
         ],
@@ -483,7 +511,7 @@
         ),
         name="exchange",
     )(tokens, cotangent, routes.T, gates.T, expert_weights)
-    pieces = max(1, devices // 4)
+    pieces = max(1, blocks // 4)
     slots = 5
     return pl.pallas_call(
         functools.partial(outer_kernel, pieces, length),
@@ -492,9 +520,9 @@
         out_specs=any_space,
         scratch_shapes=[
             pltpu.VMEM((local, parts, hidden, padded), jnp.bfloat16),
-            pltpu.VMEM((local, devices, 2, padded, features), jnp.bfloat16),
-            pltpu.VMEM((slots, parts, hidden, pieces * features), jnp.bfloat16),
-            pltpu.SemaphoreType.DMA((local * (devices // pieces),)),
+            pltpu.VMEM((local, blocks, 2, padded, columns), jnp.bfloat16),
+            pltpu.VMEM((slots, parts, hidden, pieces * columns), jnp.bfloat16),
+            pltpu.SemaphoreType.DMA((local * (blocks // pieces),)),
             pltpu.SemaphoreType.DMA((slots,)),
             pltpu.SemaphoreType.DMA((local,)),
         ],

time: 61.8 us -> 66 us (1.068)
  Pallas kernels: 61.6 us -> 65.8 us
    pallas_call x1, Pallas kernels: 49.2 us -> 53.4 us  [per_device(): pl.pallas_call(functools.partial(exchange_kernel, sizes), out_shape=(jax....]
where the time goes in v5:
time: 66 us; the launch traced here: 65.8 us
  Pallas kernels  65.8 us (100%)
    pallas_call x1, Pallas kernels, per_device(): pl.pallas_call(functools.partial(exchange_kernel, sizes), out_shape=(jax....  53.4 us
    pallas_call x1, Pallas kernels, per_device(): pl.pallas_call(functools.partial(outer_kernel, pieces, length), out_shape...  12.4 us

profile of v5, /device:TPU:0, one launch (start us, length us, event | category | flops | bytes accessed | tf_op | source)
XLA Modules:
  0.0 65.8 jit_solution(18043037265061910007)
XLA Ops:
  0.0 53.4 %exchange.1 = (bf16[16,2,4,160,256]{4,3,2,1,0:T(8,128)(2,1)}, bf16[4,3,256,256]{3,2,1,0:T(8,128)(2,1)}) custom-call(bf16[128,512]{1,0:T(8,128)(2,1)} %tok_ref.1, bf16[128,512]{1,0:T(8,128)(2,1)} %cot_ref.1, s32[2,128]{1,0:T(2,128)} %bitcast.2, f32[2,128]{1,0:T(2,128)} %bitcast.3, bf16[4,3,256,4096]{3,2,1,0:T(8,128)(2,1)} %w_ref.1), custom_call_target="tpu_custom_call" | custom-call | tf_op jit(solution)/shard_map/exchange/pallas_call | solution.py:481
  53.4 12.4 %outer.1 = bf16[4,3,256,4096]{3,2,1,0:T(8,128)(2,1)} custom-call(bf16[4,3,256,256]{3,2,1,0:T(8,128)(2,1)} %get-tuple-element.7.pre_hbm, bf16[16,2,4,160,256]{4,3,2,1,0:T(8,128)(2,1)} %get-tuple-element.8.rows_ref), custom_call_target="tpu_custom_call" | custom-call | tf_op jit(solution)/shard_map/outer/pallas_call | solution.py:516
